TPU v7x, 32 devices: a whole 2x2x4 slice. The times are simulated.
32 devices in a mesh: groups: 2 (over x), tm: 16 (over z, y, core).
Axes of the slice: x: 2, y: 2, z: 4, core: 2. Of those that a mesh axis runs over, the one named last changes fastest.
Arguments:
- sharded_latents: bfloat16 [32, 6144], P('groups', 'tm'), parts along dimension 0, may hold values from -6 to 6
- sample_frame_count: int32 [16], P('groups'), parts along dimension 0, may hold values from 5 to 8, as said below
- entry_kernel: bfloat16 [27, 16, 384], replicated, may hold values from -0.3125 to 0.3125
- entry_bias: float32 [384], replicated, may hold values from -3 to 3
- norm_scale_gain: float32 [384], replicated, may hold values from 0.25 to 1.75
- residual_kernel: bfloat16 [27, 384, 384], P(None, 'tm'), may hold values from -0.0625 to 0.0625
- residual_bias: float32 [384], replicated, may hold values from -3 to 3
Outputs:
- decoded: bfloat16 [128, 6, 16, 384], P(('groups', 'tm')), parts along dimension 0
There are 2 independent parts, one for each index of `groups`. A program takes and returns all parts, laid end to end along the dimension named above; an argument that names none is the same for every part. Nothing has to cross between parts.
Inputs may be any that keep to these rules, and one draw needn't show every extreme that they name: `sample_frame_count`: every sample has more than half of its 8 frames valid; some sample has all of them valid.
All inputs are finite; a program needn't handle non-finite values.
Results may differ from a plain program's by a relative error of at most 0.009.
Values may be sent and summed in bfloat16 or wider, within the bound.
A program may use at most 64 MiB of HBM per device.

v0:
```python
import jax
import jax.numpy as jnp
from jax import lax
from jax.sharding import PartitionSpec as P

LATENT_CHANNELS = 16
C = 384
PROMPT_SAMPLES = 8
BLOCK_FRAMES = 4
LATENT_ROWS = 6
LATENT_COLUMNS = 16


def from_behind(block, axis, distance):
    devices = range(lax.axis_size(axis))
    route = [(i - distance, i) for i in devices if i - distance in devices]
    return lax.ppermute(block, axis, route)


def causal_conv(frames, weight):
    frames_out = frames.shape[0] - 2
    inputs = frames.shape[3]
    padded = jnp.pad(frames, ((0, 0), (1, 1), (1, 1), (0, 0)))
    total = jnp.zeros((frames_out * LATENT_ROWS * LATENT_COLUMNS, weight.shape[2]), jnp.float32)
    for time_tap in range(3):
        for row_tap in range(3):
            for col_tap in range(3):
                window = padded[
                    time_tap : time_tap + frames_out,
                    row_tap : row_tap + LATENT_ROWS,
                    col_tap : col_tap + LATENT_COLUMNS,
                    :,
                ]
                window = window.reshape(frames_out * LATENT_ROWS * LATENT_COLUMNS, inputs)
                tap = 9 * time_tap + 3 * row_tap + col_tap
                total = total + jnp.dot(window, weight[tap], preferred_element_type=jnp.float32)
    return total


def activate(stream, norm_scale_gain):
    values = stream.astype(jnp.float32)
    scale = lax.rsqrt(jnp.mean(values * values, axis=-1, keepdims=True) + 1e-06)
    return jax.nn.silu(values * scale * norm_scale_gain).astype(jnp.bfloat16)


def to_cells(planes):
    return jnp.transpose(
        planes.reshape(planes.shape[0], LATENT_CHANNELS, LATENT_ROWS, LATENT_COLUMNS), (0, 2, 3, 1)
    )


def shards(
    sharded_latents,
    sample_frame_count,
    entry_kernel,
    entry_bias,
    norm_scale_gain,
    residual_kernel,
    residual_bias,
):
    gathered_latents = lax.all_to_all(
        sharded_latents, "tm", split_axis=0, concat_axis=1, tiled=True
    )
    latent_volume = gathered_latents.reshape(
        BLOCK_FRAMES, LATENT_CHANNELS, LATENT_ROWS * LATENT_COLUMNS
    )
    position = lax.axis_index("tm")
    block = position // PROMPT_SAMPLES
    sample = position % PROMPT_SAMPLES
    keep = block > 0
    earlier = from_behind(latent_volume, "tm", PROMPT_SAMPLES)
    earlier = jnp.where(keep, earlier, jnp.zeros_like(earlier))
    frames = to_cells(jnp.concatenate([earlier, latent_volume], axis=0))
    widened = (causal_conv(frames, entry_kernel) + entry_bias).astype(jnp.bfloat16)
    active_all = activate(widened, norm_scale_gain).reshape(
        BLOCK_FRAMES + 2, LATENT_ROWS, LATENT_COLUMNS, C
    )
    behind = jnp.where(keep, active_all[:2], jnp.zeros_like(active_all[:2]))
    extended = jnp.concatenate([behind, active_all[2:]], axis=0)
    stream = widened[2 * LATENT_ROWS * LATENT_COLUMNS :]
    kernel_all = lax.all_gather(residual_kernel, "tm", axis=1, tiled=True)
    branch = causal_conv(extended, kernel_all)
    total = (stream.astype(jnp.float32) + (branch + residual_bias)).reshape(
        BLOCK_FRAMES, LATENT_ROWS, LATENT_COLUMNS, C
    )
    limit = jnp.sum(jnp.where(jnp.arange(PROMPT_SAMPLES) == sample, sample_frame_count, 0))
    frame_index = block * BLOCK_FRAMES + jnp.arange(BLOCK_FRAMES)
    valid = (frame_index < limit)[:, None, None, None]
    return jnp.where(valid, total, jnp.zeros_like(total)).astype(jnp.bfloat16)


def solution(mesh):
    in_specs = (P("groups", "tm"), P("groups"), P(), P(), P(), P(None, "tm", None), P())
    out_specs = P(("groups", "tm"), None, None, None)
    return jax.shard_map(shards, mesh=mesh, in_specs=in_specs, out_specs=out_specs, check_vma=False)
```

profile of v0, /device:TPU:0, one launch (start us, length us, event | category | flops | bytes accessed | tf_op | source)
XLA Modules:
  0.0 109.1 jit_solution(9590959347050248216)
XLA Ops:
  6.5 0.7 all-gather.2.cloned.1.call-update
  7.3 0.5 broadcast.36
  7.8 1.4 %reduce.2 = bf16[16,384]{1,0:T(8,128)(2,1)S(1)} reduce(bf16[16,1,384]{2,0,1:T(8,128)(2,1)} %bitcast.334, bf16[]{:T(256)} %broadcast.36), dimensions={1}, to_apply=%copy.62.reduce_sub_computation | reduce | bytes 24578 | tf_op jit(solution)/shard_map/all_to_all | solution.py:61
  9.1 0.7 reshape.257
  9.8 7.4 %all-to-all-start = ((bf16[16,2,192]{2,1,0:T(2,128)(2,1)}), bf16[16,2,192]{2,1,0:T(2,128)(2,1)S(1)}, u32[]{:S(2)}, u32[]{:S(2)}) async-start(bf16[16,2,192]{2,1,0:T(2,128)(2,1)} %reshape.257), calls=%async_computation | async-start | bytes 32768 | tf_op jit(solution)/shard_map/all_to_all | solution.py:61
  17.2 1.3 %fusion.70 = s32[]{:T(128)} fusion(s32[8]{0:T(128)} %param.8, s32[]{:T(128)S(6)} %select_n.39), kind=kLoop, calls=%fused_computation.186 | loop fusion | flops 23 | bytes 40 | tf_op jit(solution)/shard_map/reduce_sum | solution.py:86
  18.5 5.2 %all-to-all-done = bf16[16,2,192]{2,1,0:T(2,128)(2,1)S(1)} async-done(((bf16[16,2,192]{2,1,0:T(2,128)(2,1)}), bf16[16,2,192]{2,1,0:T(2,128)(2,1)S(1)}, u32[]{:S(2)}, u32[]{:S(2)}) %all-to-all-start) | async-done | bytes 12320 | tf_op jit(solution)/shard_map/all_to_all | solution.py:61
  24.0 2.4 %collective-permute-start = (bf16[4,16,96]{2,1,0:T(8,128)(2,1)S(1)}, bf16[4,16,96]{2,1,0:T(8,128)(2,1)S(1)}, u32[]{:S(2)}, u32[]{:S(2)}) collective-permute-start(bf16[4,16,96]{2,1,0:T(8,128)(2,1)S(1)} %reshape.200), channel_id=1, source_target_pairs={{0,8},{1,9},{2,10},{3,11},{4,12},{5,13},{6,14},{7,15},{16,24},{17,... | collective-permute-start | bytes 36872 | tf_op jit(solution)/shard_map/ppermute | solution.py:17
  26.4 0.6 add_compare_fusion
  27.2 0.7 collective-permute-done
  28.1 0.4 pad_slice_fusion.30
  28.5 0.8 reshape.201
  29.3 0.6 pad_slice_fusion.28
  29.9 0.8 reshape.202
  30.7 0.8 reshape.203
  31.6 0.8 reshape.204
  32.4 0.8 reshape.205
  33.2 0.8 reshape.206
  34.0 0.8 reshape.207
  34.8 0.8 reshape.208
  35.7 0.8 reshape.209
  36.5 0.8 reshape.210
  37.3 0.5 pad_slice_fusion.29
  37.9 0.8 reshape.211
  38.7 0.8 reshape.212
  42.8 1.0 fusion.41
  43.8 1.0 convolution_add_fusion.25
  44.9 1.1 convolution_add_fusion.24
  52.1 0.5 convolution_add_fusion.4
  53.6 0.4 fusion.4
  54.5 0.9 fusion.13
  55.4 1.2 %pad_slice_fusion.1 = (bf16[4,6,16,384]{3,2,1,0:T(8,128)(2,1)}, bf16[4,6,16,384]{3,2,1,0:T(8,128)(2,1)}, bf16[4,6,16,384]{3,2,1,0:T(8,128)(2,1)}, bf16[4,6,16,384]{3,2,1,0:T(8,128)(2,1)}, bf16[4,6,16,384]{3,2,1,0:T(8,128)(2,1)}) fusion(bf16[6,6,16,384]{3,2,1,0:T(8,128)(2,1)S(1)} %pad_maximum_fusion), kind=kLoop, calls=%fused_computation.1 | loop fusion | bytes 1916928 | tf_op jit(solution)/shard_map/slice | solution.py:28
  56.6 2.2 %pad_slice_fusion = (bf16[4,6,16,384]{3,2,1,0:T(8,128)(2,1)}, bf16[4,6,16,384]{3,2,1,0:T(8,128)(2,1)}, bf16[4,6,16,384]{3,2,1,0:T(8,128)(2,1)}, bf16[4,6,16,384]...) fusion(bf16[6,6,16,384]{3,2,1,0:T(8,128)(2,1)S(1)} %pad_maximum, ...), kind=kLoop, calls=%fused_computation | loop fusion | bytes 6045696 | tf_op jit(solution)/shard_map/slice | solution.py:28
  58.8 26.1 %all-gather.2.cloned.1.call-done = bf16[27,384,384]{2,1,0:T(8,128)(2,1)} async-done(((bf16[27,24,384]{2,1,0:T(8,128)(2,1)}), bf16[27,384,384]{2,1,0:T(8,128)(2,1)}) %all-gather.2.cloned.1.call-update) | async-done | bytes 7962640 | tf_op jit(solution)/shard_map/all_gather | solution.py:81
  84.9 1.5 %fusion.14 = f32[384,384]{1,0:T(8,128)S(1)} fusion(bf16[384,384]{1,0:T(8,128)(2,1)} %bitcast.333, bf16[27,384,384]{2,1,0:T(8,128)(2,1)} %all-gather.2.cloned.1.call-done), kind=kOutput, calls=%fused_computation.125 | convolution fusion | flops 113246208 | bytes 1179648 | tf_op jit(solution)/shard_map/dot_general | solution.py:36
  86.5 2.0 %convolution_add_fusion.51 = f32[384,384]{1,0:T(8,128)S(1)} fusion(f32[384,384]{1,0:T(8,128)S(1)} %fusion.14, bf16[384,384]{1,0:T(8,128)(2,1)} %bitcast.324, bf16[27,384,384]{2,1,0:T(8,128)(2,1)} %all-gather.2.cloned.1.call-done), kind=kOutput, calls=%fused_computation.79 | convolution fusion | flops 113393664 | bytes 1769472 | tf_op jit(solution)/shard_map/dot_general | solution.py:36
  88.5 1.4 %convolution_add_fusion.50 = f32[384,384]{1,0:T(8,128)S(1)} fusion(f32[384,384]{1,0:T(8,128)S(1)} %convolution_add_fusion.51, bf16[384,384]{1,0:T(8,128)(2,1)} %bitcast.323, bf16[27,384,384]{2,1,0:T(8,128)(2,1)} %all-gather.2.cloned.1.call-done), kind=kOutput, calls=%fused_computation.78 | convolution fusion | flops 113393664 | bytes 1769472 | tf_op jit(solution)/shard_map/dot_general | solution.py:36
  89.9 1.4 %convolution_add_fusion.49 = f32[384,384]{1,0:T(8,128)S(1)} fusion(f32[384,384]{1,0:T(8,128)S(1)} %convolution_add_fusion.50, bf16[384,384]{1,0:T(8,128)(2,1)} %bitcast.322, bf16[27,384,384]{2,1,0:T(8,128)(2,1)} %all-gather.2.cloned.1.call-done), kind=kOutput, calls=%fused_computation.77 | convolution fusion | flops 113393664 | bytes 1769472 | tf_op jit(solution)/shard_map/dot_general | solution.py:36
  91.3 1.4 %convolution_add_fusion.48 = f32[384,384]{1,0:T(8,128)S(1)} fusion(f32[384,384]{1,0:T(8,128)S(1)} %convolution_add_fusion.49, bf16[384,384]{1,0:T(8,128)(2,1)} %bitcast.327, bf16[27,384,384]{2,1,0:T(8,128)(2,1)} %all-gather.2.cloned.1.call-done), kind=kOutput, calls=%fused_computation.76 | convolution fusion | flops 113393664 | bytes 1769472 | tf_op jit(solution)/shard_map/dot_general | solution.py:36
  92.7 1.3 %convolution_add_fusion.47 = f32[384,384]{1,0:T(8,128)S(1)} fusion(f32[384,384]{1,0:T(8,128)S(1)} %convolution_add_fusion.48, bf16[384,384]{1,0:T(8,128)(2,1)} %bitcast.321, bf16[27,384,384]{2,1,0:T(8,128)(2,1)S(1)} %copy-done), kind=kOutput, calls=%fused_computation.75 | convolution fusion | flops 113393664 | bytes 1769472 | tf_op jit(solution)/shard_map/dot_general | solution.py:36
  95.8 0.3 convolution_add_fusion.41
  96.1 0.3 convolution_add_fusion.40
  96.8 0.3 convolution_add_fusion.38
  97.2 0.3 convolution_add_fusion.37
  97.5 0.3 convolution_add_fusion.36
  97.9 0.3 convolution_add_fusion.35
  101.0 0.4 fusion.3
  101.4 0.8 select_convert_fusion
  (141 shorter events, 16.2 us)
Async XLA Ops:
  6.5 78.4 %all-gather.2.cloned.1.call-start = ((), (), s32[]{:S(2)}) async-start(), calls=%async_computation.1 | async-start | bytes 8460288 | tf_op jit(solution)/shard_map/all_gather | solution.py:81
  9.8 13.9 %all-to-all-start = ((bf16[16,2,192]{2,1,0:T(2,128)(2,1)}), bf16[16,2,192]{2,1,0:T(2,128)(2,1)S(1)}, u32[]{:S(2)}, u32[]{:S(2)}) async-start(bf16[16,2,192]{2,1,0:T(2,128)(2,1)} %reshape.257), calls=%async_computation | async-start | bytes 32768 | tf_op jit(solution)/shard_map/all_to_all | solution.py:61
  24.0 3.9 %collective-permute-start = (bf16[4,16,96]{2,1,0:T(8,128)(2,1)S(1)}, bf16[4,16,96]{2,1,0:T(8,128)(2,1)S(1)}, u32[]{:S(2)}, u32[]{:S(2)}) collective-permute-start(bf16[4,16,96]{2,1,0:T(8,128)(2,1)S(1)} %reshape.200), channel_id=1, source_target_pairs={{0,8},{1,9},{2,10},{3,11},{4,12},{5,13},{6,14},{7,15},{16,24},{17,... | collective-permute-start | bytes 36872 | tf_op jit(solution)/shard_map/ppermute | solution.py:17
  37.8 8.2 %copy-start.13 = (bf16[576,16]{0,1:T(8,128)(2,1)S(1)}, bf16[576,16]{0,1:T(8,128)(2,1)}, u32[]{:S(2)}) copy-start(bf16[576,16]{0,1:T(8,128)(2,1)} %reshape.204) | copy-start | bytes 55300
  38.6 7.7 %copy-start.14 = (bf16[576,16]{0,1:T(8,128)(2,1)S(1)}, bf16[576,16]{0,1:T(8,128)(2,1)}, u32[]{:S(2)}) copy-start(bf16[576,16]{0,1:T(8,128)(2,1)} %reshape.205) | copy-start | bytes 55300
  38.7 4.1 %copy-start.12 = (bf16[27,16,384]{2,1,0:T(8,128)(2,1)S(1)}, bf16[27,16,384]{2,1,0:T(8,128)(2,1)}, u32[]{:S(2)}) copy-start(bf16[27,16,384]{2,1,0:T(8,128)(2,1)} %param.9) | copy-start | bytes 995332
  39.9 6.7 %copy-start.15 = (bf16[576,16]{0,1:T(8,128)(2,1)S(1)}, bf16[576,16]{0,1:T(8,128)(2,1)}, u32[]{:S(2)}) copy-start(bf16[576,16]{0,1:T(8,128)(2,1)} %reshape.206) | copy-start | bytes 55300
  40.6 6.4 %copy-start.16 = (bf16[576,16]{0,1:T(8,128)(2,1)S(1)}, bf16[576,16]{0,1:T(8,128)(2,1)}, u32[]{:S(2)}) copy-start(bf16[576,16]{0,1:T(8,128)(2,1)} %reshape.207) | copy-start | bytes 55300
  41.2 6.1 %copy-start.17 = (bf16[576,16]{0,1:T(8,128)(2,1)S(1)}, bf16[576,16]{0,1:T(8,128)(2,1)}, u32[]{:S(2)}) copy-start(bf16[576,16]{0,1:T(8,128)(2,1)} %reshape.208) | copy-start | bytes 55300
  41.9 5.7 %copy-start.18 = (bf16[576,16]{0,1:T(8,128)(2,1)S(1)}, bf16[576,16]{0,1:T(8,128)(2,1)}, u32[]{:S(2)}) copy-start(bf16[576,16]{0,1:T(8,128)(2,1)} %reshape.209) | copy-start | bytes 55300
  42.5 5.4 %copy-start.19 = (bf16[576,16]{0,1:T(8,128)(2,1)S(1)}, bf16[576,16]{0,1:T(8,128)(2,1)}, u32[]{:S(2)}) copy-start(bf16[576,16]{0,1:T(8,128)(2,1)} %reshape.210) | copy-start | bytes 55300
  43.8 4.4 %copy-start.20 = (bf16[576,16]{0,1:T(8,128)(2,1)S(1)}, bf16[576,16]{0,1:T(8,128)(2,1)}, u32[]{:S(2)}) copy-start(bf16[576,16]{0,1:T(8,128)(2,1)} %reshape.211) | copy-start | bytes 55300
  44.9 3.7 %copy-start.21 = (bf16[576,16]{0,1:T(8,128)(2,1)S(1)}, bf16[576,16]{0,1:T(8,128)(2,1)}, u32[]{:S(2)}) copy-start(bf16[576,16]{0,1:T(8,128)(2,1)} %reshape.212) | copy-start | bytes 55300
  50.5 3.1 %copy-start.22 = (f32[384]{0:T(512)S(1)}, f32[384]{0:T(512)}, u32[]{:S(2)}) copy-start(f32[384]{0:T(512)} %param.10) | copy-start | bytes 4612
  50.8 3.2 %copy-start.23 = (f32[384]{0:T(512)S(1)}, f32[384]{0:T(512)}, u32[]{:S(2)}) copy-start(f32[384]{0:T(512)} %param.11) | copy-start | bytes 4612
  84.9 7.8 %copy-start = (bf16[27,384,384]{2,1,0:T(8,128)(2,1)S(1)}, bf16[27,384,384]{2,1,0:T(8,128)(2,1)}, u32[]{:S(2)}) copy-start(bf16[27,384,384]{2,1,0:T(8,128)(2,1)} %all-gather.2.cloned.1.call-done) | copy-start | bytes 23887876
  84.9 9.1 %copy-start.5 = (bf16[4,6,16,384]{3,2,1,0:T(8,128)(2,1)S(1)}, bf16[4,6,16,384]{3,2,1,0:T(8,128)(2,1)}, u32[]{:S(2)}) copy-start(bf16[4,6,16,384]{3,2,1,0:T(8,128)(2,1)} %get-tuple-element.10) | copy-start | bytes 884740
  84.9 9.5 %copy-start.4 = (bf16[4,6,16,384]{3,2,1,0:T(8,128)(2,1)S(1)}, bf16[4,6,16,384]{3,2,1,0:T(8,128)(2,1)}, u32[]{:S(2)}) copy-start(bf16[4,6,16,384]{3,2,1,0:T(8,128)(2,1)} %get-tuple-element.11) | copy-start | bytes 884740
  84.9 9.8 %copy-start.3 = (bf16[4,6,16,384]{3,2,1,0:T(8,128)(2,1)S(1)}, bf16[4,6,16,384]{3,2,1,0:T(8,128)(2,1)}, u32[]{:S(2)}) copy-start(bf16[4,6,16,384]{3,2,1,0:T(8,128)(2,1)} %get-tuple-element.12) | copy-start | bytes 884740
  84.9 10.2 %copy-start.2 = (bf16[4,6,16,384]{3,2,1,0:T(8,128)(2,1)S(1)}, bf16[4,6,16,384]{3,2,1,0:T(8,128)(2,1)}, u32[]{:S(2)}) copy-start(bf16[4,6,16,384]{3,2,1,0:T(8,128)(2,1)} %get-tuple-element.13) | copy-start | bytes 884740
  86.4 9.0 %copy-start.1 = (bf16[4,6,16,384]{3,2,1,0:T(8,128)(2,1)S(1)}, bf16[4,6,16,384]{3,2,1,0:T(8,128)(2,1)}, u32[]{:S(2)}) copy-start(bf16[4,6,16,384]{3,2,1,0:T(8,128)(2,1)} %get-tuple-element.14) | copy-start | bytes 884740
  91.3 5.2 %copy-start.7 = (bf16[4,6,16,384]{3,2,1,0:T(8,128)(2,1)S(1)}, bf16[4,6,16,384]{3,2,1,0:T(8,128)(2,1)}, u32[]{:S(2)}) copy-start(bf16[4,6,16,384]{3,2,1,0:T(8,128)(2,1)} %get-tuple-element.29) | copy-start | bytes 884740
  96.1 3.1 %copy-start.11 = (bf16[4,6,16,384]{3,2,1,0:T(8,128)(2,1)S(1)}, bf16[4,6,16,384]{3,2,1,0:T(8,128)(2,1)}, u32[]{:S(2)}) copy-start(bf16[4,6,16,384]{3,2,1,0:T(8,128)(2,1)} %get-tuple-element.25) | copy-start | bytes 884740
  96.8 3.1 %copy-start.10 = (bf16[4,6,16,384]{3,2,1,0:T(8,128)(2,1)S(1)}, bf16[4,6,16,384]{3,2,1,0:T(8,128)(2,1)}, u32[]{:S(2)}) copy-start(bf16[4,6,16,384]{3,2,1,0:T(8,128)(2,1)} %get-tuple-element.26) | copy-start | bytes 884740
  97.2 3.1 %copy-start.9 = (bf16[4,6,16,384]{3,2,1,0:T(8,128)(2,1)S(1)}, bf16[4,6,16,384]{3,2,1,0:T(8,128)(2,1)}, u32[]{:S(2)}) copy-start(bf16[4,6,16,384]{3,2,1,0:T(8,128)(2,1)} %get-tuple-element.27) | copy-start | bytes 884740
  97.5 3.1 %copy-start.8 = (bf16[4,6,16,384]{3,2,1,0:T(8,128)(2,1)S(1)}, bf16[4,6,16,384]{3,2,1,0:T(8,128)(2,1)}, u32[]{:S(2)}) copy-start(bf16[4,6,16,384]{3,2,1,0:T(8,128)(2,1)} %get-tuple-element.24) | copy-start | bytes 884740
  97.9 3.1 %copy-start.6 = (bf16[4,6,16,384]{3,2,1,0:T(8,128)(2,1)S(1)}, bf16[4,6,16,384]{3,2,1,0:T(8,128)(2,1)}, u32[]{:S(2)}) copy-start(bf16[4,6,16,384]{3,2,1,0:T(8,128)(2,1)} %get-tuple-element.5) | copy-start | bytes 884740
  97.9 3.1 %copy-start.24 = (f32[384]{0:T(512)S(1)}, f32[384]{0:T(512)}, u32[]{:S(2)}) copy-start(f32[384]{0:T(512)} %param.13) | copy-start | bytes 4612
Sparse Core Ops, SparseCore 0:
  9.5 75.3 all-gather.1
where the time goes:
time: 110 us; the launch traced here: 109 us
  waiting for transfers between devices  32.7 us (30%)
  matrix products  27 us (25%)
  local copies, waits for them, and re-layouts  19.7 us (18%)
  between operations  14.4 us (13%)
  starting transfers between devices  9.76 us (9%)
  other arithmetic  5.58 us (5%)
    dot_general x54, matrix products, causal_conv(): jnp.dot(window, weight[tap], preferred_element_type=jnp.float32)  27 us
    all_gather x1, waiting for transfers between devices, shards(): kernel_all = lax.all_gather(residual_kernel, 'tm', axis=1, tiled=True)  26.1 us
    reshape x27, local copies, waits for them, and re-layouts, causal_conv(): window = window.reshape(frames_out * LATENT_ROWS * LATENT_COLUMNS, inputs)  12 us
    all_to_all x1, starting transfers between devices, shards(): lax.all_to_all(sharded_latents, 'tm', split_axis=0, concat_axis=1, tiled=...  7.39 us
    slice x32, local copies, waits for them, and re-layouts, causal_conv(): padded[time_tap:time_tap + frames_out, row_tap:row_tap + LATENT_ROWS, col...  5.87 us
    all_to_all x1, waiting for transfers between devices, shards(): lax.all_to_all(sharded_latents, 'tm', split_axis=0, concat_axis=1, tiled=...  5.18 us
    ppermute x1, starting transfers between devices, from_behind(): return lax.ppermute(block, axis, route)  2.37 us
  transfers between devices with their start and end apart: 3, of which 3 were waited for; matrix products, arithmetic and copies ran while one was open for 32% of the time, Pallas kernels for 0%

commit v1 on v0

--- a/solution.py
+++ b/solution.py
@@ -1,6 +1,9 @@
 import jax
 import jax.numpy as jnp
+import numpy as np
 from jax import lax
+from jax.experimental import pallas as pl
+from jax.experimental.pallas import tpu as pltpu
 from jax.sharding import PartitionSpec as P
 
 LATENT_CHANNELS = 16
@@ -89,7 +92,317 @@
     return jnp.where(valid, total, jnp.zeros_like(total)).astype(jnp.bfloat16)
 
 
+MESH = pl.DeviceIdType.MESH
+F32, BF16 = jnp.float32, jnp.bfloat16
+CELLS = LATENT_ROWS * LATENT_COLUMNS
+PLANE = 128
+SLICES = 3
+TAPS = 7
+
+
+def section_kernel(
+    latq, perm, mask, entry, entry_bias, gain, residual_bias, pieces,
+    out,
+    lat, at, act, kept, weights, acc, done,
+    lat_send, lat_recv, z_send, z_recv, p_send, p_recv, c_send, c_recv, o_send, o_recv, own,
+):
+    x = lax.axis_index("groups")
+    me = lax.axis_index("tm")
+    z, y, c = me // 4, (me // 2) % 2, me % 2
+    quarter = 2 * x + c
+    across = 2 * (1 - x) + c
+
+    def where_(zz, yy, cc):
+        return {"tm": zz * 4 + yy * 2 + cc}
+
+    peers = [
+        {"groups": x, "tm": z * 4 + (1 - y) * 2 + c},
+        {"groups": 1 - x, "tm": me},
+        {"groups": 1 - x, "tm": z * 4 + (1 - y) * 2 + c},
+    ]
+    sibling = {"tm": z * 4 + y * 2 + (1 - c)}
+
+    barrier = pltpu.get_barrier_semaphore()
+    for step in range(1, 16):
+        pl.semaphore_signal(barrier, inc=1, device_id={"tm": lax.rem(me + step, 16)}, device_id_type=MESH)
+    for peer in peers[1:]:
+        pl.semaphore_signal(barrier, inc=1, device_id=peer, device_id_type=MESH)
+    pl.semaphore_wait(barrier, 17)
+
+    def remote(src, dst, send, recv, device):
+        return pltpu.make_async_remote_copy(
+            src_ref=src, dst_ref=dst, send_sem=send, recv_sem=recv, device_id=device, device_id_type=MESH
+        )
+
+    def lat_copy(to):
+        return remote(latq.at[to % 4], lat.at[me], lat_send.at[to], lat_recv.at[me], {"tm": to})
+
+    def rows_of(zz, yy):
+        return pl.ds(pl.multiple_of(48 * (2 * zz + yy), 16), 48)
+
+    def z_copy(n):
+        return remote(
+            pieces.at[n], weights.at[quarter, :, rows_of(z, y), :], z_send.at[n], z_recv.at[z], where_(n, y, c)
+        )
+
+    def z_arrival(zz):
+        return remote(
+            pieces.at[0], weights.at[quarter, :, rows_of(zz, y), :], z_send.at[0], z_recv.at[zz], where_(zz, y, c)
+        )
+
+    def p_copy(r, zz):
+        block = weights.at[quarter, :, rows_of(zz, y), :]
+        return remote(block, block, p_send.at[r, zz], p_recv.at[r, zz], peers[r])
+
+    def p_arrival(r, zz):
+        block = weights.at[quarter if r == 0 else across, :, rows_of(zz, y if r == 1 else 1 - y), :]
+        return remote(block, block, p_send.at[r, zz], p_recv.at[r, zz], peers[r])
+
+    def c_copy(i):
+        block = weights.at[quarter if i == 0 else across]
+        return remote(block, block, c_send.at[i], c_recv.at[i], sibling)
+
+    def c_arrival(i):
+        block = weights.at[2 * x + 1 - c if i == 0 else 2 * (1 - x) + 1 - c]
+        return remote(block, block, c_send.at[i], c_recv.at[i], sibling)
+
+    def columns(n):
+        return pl.ds(pl.multiple_of(128 * n, 128), 128)
+
+    def o_copy(d):
+        return remote(done.at[d], out.at[:, columns(z)], o_send.at[d], o_recv.at[z], where_(d, y, c))
+
+    def o_arrival(n):
+        return remote(done.at[0], out.at[:, columns(n)], o_send.at[0], o_recv.at[n], where_(n, y, c))
+
+    for to in range(12):
+        @pl.when(to != me)
+        def _():
+            lat_copy(to).start()
+
+    for n in range(SLICES):
+        @pl.when(n != z)
+        def _():
+            z_copy(n).start()
+
+    @pl.when(z < SLICES)
+    def _():
+        mine = [
+            pltpu.make_async_copy(latq.at[me % 4], lat.at[me], own.at[0]),
+            pltpu.make_async_copy(pieces.at[lax.rem(z, SLICES)], weights.at[quarter, :, rows_of(z, y), :], own.at[1]),
+        ]
+        for copy in mine:
+            copy.start()
+        at[:, 0:2] = jnp.zeros((2, 2, 144, PLANE), BF16)
+        act[:, :, 0:2] = jnp.zeros((3, 2, 2, PLANE, C), BF16)
+        act[:, :, 2:, 0:16] = jnp.zeros((3, 2, 8, 16, C), BF16)
+        act[:, :, 2:, 112:128] = jnp.zeros((3, 2, 8, 16, C), BF16)
+        mine[0].wait()
+        for source in range(16):
+            @pl.when(source != me)
+            def _():
+                remote(latq.at[0], lat.at[source], lat_send.at[0], lat_recv.at[source], {"tm": source}).wait_recv()
+        cells = jnp.dot(perm[...], lat[...].reshape(256, PLANE), preferred_element_type=F32)
+        lane = lax.broadcasted_iota(jnp.int32, (256, PLANE), 1)
+        row, column = lane // LATENT_COLUMNS, lane % LATENT_COLUMNS
+        for j in range(3):
+            for k in range(3):
+                offset = (j - 1) * LATENT_COLUMNS + (k - 1)
+                moved = pltpu.roll(cells, (-offset) % PLANE, 1) if offset else cells
+                good = (
+                    (row + (j - 1) >= 0)
+                    & (row + (j - 1) < LATENT_ROWS)
+                    & (column + (k - 1) >= 0)
+                    & (column + (k - 1) < LATENT_COLUMNS)
+                )
+                tap = 3 * j + k
+                at[:, 2:, tap * 16 : tap * 16 + 16, :] = (
+                    jnp.where(good, moved, 0.0).astype(BF16).reshape(2, 8, 16, PLANE)
+                )
+
+        def inlet(index, carry):
+            h, f = index // 8, index % 8
+            left = at[h, pl.ds(f, 3)].reshape(432, PLANE)
+            wide = lax.dot_general(left, entry[...], (((0,), (0,)), ((), ())), preferred_element_type=F32)
+            stream = (wide[:CELLS] + entry_bias[...]).astype(BF16)
+            kept[index] = stream
+            values = stream.astype(F32)
+            scale = lax.rsqrt(jnp.mean(values * values, axis=-1, keepdims=True) + 1e-06)
+            u = values * scale * gain[...]
+            active = (u / (1.0 + jnp.exp(-u))).astype(BF16).astype(F32)
+            column = lax.broadcasted_iota(jnp.int32, (CELLS, C), 0) % LATENT_COLUMNS
+            act[1, h, 2 + f, 16:112] = active.astype(BF16)
+            act[0, h, 2 + f, 16:112] = jnp.where(column == 0, 0.0, pltpu.roll(active, 1, 0)).astype(BF16)
+            act[2, h, 2 + f, 16:112] = jnp.where(
+                column == LATENT_COLUMNS - 1, 0.0, pltpu.roll(active, CELLS - 1, 0)
+            ).astype(BF16)
+            return carry
+
+        lax.fori_loop(0, 8, inlet, 0)
+        mine[1].wait()
+        for zz in range(4):
+            @pl.when(zz != z)
+            def _():
+                z_arrival(zz).wait_recv()
+            for r in range(3):
+                p_copy(r, zz).start()
+        lax.fori_loop(8, 16, inlet, 0)
+
+        def taps_of(which, d):
+            h, b = d % 2, d // 2
+
+            def step(t, total):
+                tap = jnp.minimum(which * TAPS + t, 26)
+                i, j, k = tap // 9, (tap // 3) % 3, tap % 3
+                left = act[k, h, pl.ds(4 * b + i, 4), pl.ds(pl.multiple_of(16 * j, 16), CELLS), :]
+                return total + jnp.dot(
+                    left.reshape(4 * CELLS, C), weights[which, t], preferred_element_type=F32
+                )
+
+            return step
+
+        def sweep(which, first):
+            def body(d, carry):
+                start = jnp.zeros((4 * CELLS, 128), F32) if first else acc[d]
+                acc[d] = lax.fori_loop(0, TAPS, taps_of(which, d), start, unroll=True)
+                return carry
+
+            lax.fori_loop(0, 4, body, 0)
+
+        for zz in range(4):
+            p_arrival(0, zz).wait_recv()
+        c_copy(0).start()
+        sweep(quarter, True)
+        for r in (1, 2):
+            for zz in range(4):
+                p_arrival(r, zz).wait_recv()
+        c_copy(1).start()
+        c_arrival(0).wait_recv()
+        sweep(2 * x + 1 - c, False)
+        sweep(across, False)
+        c_arrival(1).wait_recv()
+        last = 2 * (1 - x) + 1 - c
+
+        def finish(d, carry):
+            h, b = d % 2, d // 2
+            total = lax.fori_loop(0, TAPS, taps_of(last, d), acc[d], unroll=True)
+            stream = kept[pl.ds(h * 8 + b * 4, 4), :, columns(z)].astype(F32)
+            total = stream + (total + residual_bias[0:1, columns(z)]).reshape(4, CELLS, 128)
+            valid = mask[pl.ds(h * 8 + b * 4, 4)] > 0.0
+            done[d] = jnp.where(valid, total, 0.0).astype(BF16).reshape(4 * CELLS, 128)
+
+            @pl.when(d != z)
+            def _():
+                o_copy(d).start()
+
+            return carry
+
+        lax.fori_loop(0, 4, finish, 0)
+        out[:, columns(z)] = done[z]
+
+    for n in range(SLICES):
+        @pl.when(n != z)
+        def _():
+            o_arrival(n).wait_recv()
+            z_copy(n).wait_send()
+
+    for to in range(12):
+        @pl.when(to != me)
+        def _():
+            lat_copy(to).wait_send()
+
+    @pl.when(z < SLICES)
+    def _():
+        for r in range(3):
+            for zz in range(4):
+                p_copy(r, zz).wait_send()
+        for i in range(2):
+            c_copy(i).wait_send()
+        for d in range(4):
+            @pl.when(d != z)
+            def _():
+                o_copy(d).wait_send()
+
+
+def permutation():
+    matrix = np.zeros((256, 256), np.float32)
+    for h in range(2):
+        for b in range(2):
+            for g in range(4):
+                for ch in range(16):
+                    source = (g * 4 + ch // 4) * 16 + (b * 2 + h) * 4 + ch % 4
+                    matrix[(h * 8 + b * 4 + g) * 16 + ch, source] = 1.0
+    return matrix
+
+
+def sliced_shards(
+    sharded_latents,
+    sample_frame_count,
+    entry_kernel,
+    entry_bias,
+    norm_scale_gain,
+    residual_kernel,
+    residual_bias,
+):
+    x, me = lax.axis_index("groups"), lax.axis_index("tm")
+    c = me % 2
+    quarters = jnp.pad(residual_kernel, ((0, 1), (0, 0), (0, 0)))
+    mine = lax.dynamic_slice_in_dim(quarters, (2 * x + c) * TAPS, TAPS, 0)
+    theirs = lax.dynamic_slice_in_dim(quarters, (2 * x + 1 - c) * TAPS, TAPS, 0)
+    received = lax.ppermute(theirs, "tm", [(i, i ^ 1) for i in range(16)])
+    low = jnp.where(c == 0, mine, received)
+    high = jnp.where(c == 0, received, mine)
+    both = jnp.concatenate([low, high], axis=1)
+    pieces = jnp.transpose(both.reshape(TAPS, 48, SLICES, 128), (2, 0, 1, 3))
+
+    latq = jnp.transpose(sharded_latents.reshape(4, 4, 4, CELLS), (1, 0, 2, 3)).reshape(4, 16, CELLS)
+    latq = jnp.pad(latq, ((0, 0), (0, 0), (0, PLANE - CELLS)))
+    q = me % 4
+    counts = jnp.stack([
+        lax.dynamic_index_in_dim(sample_frame_count, q, keepdims=False),
+        lax.dynamic_index_in_dim(sample_frame_count, q + 4, keepdims=False),
+    ])
+    mask = (jnp.arange(8)[None, :] < counts[:, None]).astype(F32).reshape(16, 1, 1)
+    mask = jnp.broadcast_to(mask, (16, 1, 128))
+
+    vmem = pl.BlockSpec(memory_space=pltpu.VMEM)
+    dma = pltpu.SemaphoreType.DMA
+    out = pl.pallas_call(
+        section_kernel,
+        out_shape=jax.ShapeDtypeStruct((4 * CELLS, C), BF16),
+        in_specs=[vmem] * 8,
+        out_specs=vmem,
+        scratch_shapes=[
+            pltpu.VMEM((16, 16, PLANE), BF16),
+            pltpu.VMEM((2, 10, 144, PLANE), BF16),
+            pltpu.VMEM((3, 2, 10, PLANE, C), BF16),
+            pltpu.VMEM((16, CELLS, C), BF16),
+            pltpu.VMEM((4, TAPS, C, 128), BF16),
+            pltpu.VMEM((4, 4 * CELLS, 128), F32),
+            pltpu.VMEM((4, 4 * CELLS, 128), BF16),
+            dma((12,)), dma((16,)), dma((3,)), dma((4,)), dma((3, 4)), dma((3, 4)),
+            dma((2,)), dma((2,)), dma((4,)), dma((3,)), dma((2,)),
+        ],
+        compiler_params=pltpu.CompilerParams(
+            collective_id=0, has_side_effects=True, vmem_limit_bytes=40 * 1024 * 1024
+        ),
+        cost_estimate=pl.CostEstimate(flops=5_000_000_000, bytes_accessed=2_000_000, transcendentals=600_000),
+    )(
+        latq,
+        jnp.asarray(permutation(), BF16),
+        mask,
+        entry_kernel.reshape(27 * LATENT_CHANNELS, C),
+        entry_bias.reshape(1, C),
+        norm_scale_gain.reshape(1, C),
+        residual_bias.reshape(1, C),
+        pieces,
+    )
+    return out.reshape(4, LATENT_ROWS, LATENT_COLUMNS, C)
+
+
 def solution(mesh):
     in_specs = (P("groups", "tm"), P("groups"), P(), P(), P(), P(None, "tm", None), P())
     out_specs = P(("groups", "tm"), None, None, None)
-    return jax.shard_map(shards, mesh=mesh, in_specs=in_specs, out_specs=out_specs, check_vma=False)
+    sliced = mesh.shape["groups"] == 2 and mesh.shape["tm"] == 16
+    body = sliced_shards if sliced else shards
+    return jax.shard_map(body, mesh=mesh, in_specs=in_specs, out_specs=out_specs, check_vma=False)

time: 110 us -> 58.8 us (0.53)
  the two profiles are of different devices: /device:TPU:0 before, /device:TPU:26 now
where the time goes in v1:
time: 58.8 us; the launch traced here: 58.5 us
  Pallas kernels  50.8 us (86%)
  local copies, waits for them, and re-layouts  5.97 us (10%)
  other arithmetic  1.51 us (3%)
    pallas_call x1, Pallas kernels, sliced_shards(): pl.pallas_call(section_kernel, out_shape=jax.ShapeDtypeStruct((4 * CELLS,...  50.8 us
    unnamed x17, local copies, waits for them, and re-layouts  4.11 us
    another operation x1, other arithmetic, sliced_shards(): jnp.stack([lax.dynamic_index_in_dim(sample_frame_count, q, keepdims=False...  1.35 us
  transfers between devices with their start and end apart: 1, of which 0 were waited for; matrix products, arithmetic and copies ran while one was open for 4% of the time, Pallas kernels for 0%

profile of v1, /device:TPU:26, one launch (start us, length us, event | category | flops | bytes accessed | tf_op | source)
XLA Modules:
  0.0 58.5 jit_solution(10112384525421107444)
XLA Ops:
  0.0 0.0 copy-start.2
  0.0 1.0 %pad_dynamic-slice_fusion = bf16[7,24,384]{2,1,0:T(8,128)(2,1)S(1)} fusion(s32[]{:T(128)S(6)} %select_n.42, bf16[27,24,384]{2,1,0:T(8,128)(2,1)} %param.13), kind=kLoop, calls=%fused_computation | loop fusion | bytes 626692 | tf_op jit(solution)/shard_map/dynamic_slice | solution.py:351
  1.0 0.1 collective-permute-start
  1.1 0.0 copy-start.4
  1.1 0.0 copy-start.3
  1.1 0.6 %copy-done.4 = s32[8]{0:T(128)S(1)} copy-done((s32[8]{0:T(128)S(1)}, s32[8]{0:T(128)}, u32[]{:S(2)}) %copy-start.4) | copy-done | bytes 56
  1.8 0.6 %fusion = (s32[1]{0:T(128)}, s32[1]{0:T(128)}) fusion(s32[8]{0:T(128)S(1)} %copy-done.4, s32[]{:T(128)S(6)} %select_n.37, s32[]{:T(128)S(6)} %select_n.38), kind=kLoop, calls=%fused_computation.8 | loop fusion | bytes 24 | tf_op jit(solution)/shard_map/jit(dynamic_index_in_dim)/dynamic_slice | solution.py:362
  2.4 1.4 %pad_add_fusion = s32[2]{0:T(128)S(1)} fusion(s32[1]{0:T(128)} %get-tuple-element.8, s32[1]{0:T(128)} %get-tuple-element.7), kind=kLoop, calls=%fused_computation.7 | loop fusion | flops 2 | bytes 16 | tf_op jit(solution)/shard_map/stack | solution.py:361
  3.7 0.0 copy-start.5
  3.7 0.1 compare_convert_fusion
  3.8 0.1 reshape.53
  3.9 0.5 copy-done.5
  4.4 0.0 copy-start.6
  4.4 0.7 %copy-done.6 = f32[384]{0:T(512)S(1)} copy-done((f32[384]{0:T(512)S(1)}, f32[384]{0:T(512)}, u32[]{:S(2)}) %copy-start.6) | copy-done | bytes 1560
  5.1 0.0 copy-start.7
  5.1 0.7 %copy-done.7 = f32[384]{0:T(512)S(1)} copy-done((f32[384]{0:T(512)S(1)}, f32[384]{0:T(512)}, u32[]{:S(2)}) %copy-start.7) | copy-done | bytes 1560
  5.8 0.0 copy-done.3
  5.8 0.1 reshape.45
  5.9 0.0 collective-permute-done
  5.9 0.0 copy-done.2
  6.0 0.0 copy-start
  6.0 0.0 copy-start.1
  6.0 0.1 broadcast_in_dim.2.mask
  6.1 0.8 %copy-done = bf16[27,16,384]{2,1,0:T(8,128)(2,1)S(1)} copy-done((bf16[27,16,384]{2,1,0:T(8,128)(2,1)S(1)}, bf16[27,16,384]{2,1,0:T(8,128)(2,1)}, u32[]{:S(2)}) %copy-start) | copy-done | bytes 331800
  6.9 0.0 copy-done.1
  7.0 50.8 %shard_map.82 = bf16[384,384]{1,0:T(8,128)(2,1)S(1)} custom-call(bf16[4,16,128]{2,1,0:T(8,128)(2,1)S(1)} %pad.8.latq, bf16[256,256]{1,0:T(8,128)(2,1)S(1)} %copy-done.1, f32[16,1,128]{2,1,0:T(1,128)S(1)} %broadcast_in_dim.2.mask, bf16[432,384]{1,0:T(8,128)(2,1)S(1)} %bitcast.13, f32[1,384]{1,0:T(1,128)S(1)} %reshape.48.entry_bias, ...), custom_call_target="tpu_custom_call" | custom-call | flops 5000000000 | bytes 2000000 | tf_op jit(solution)/shard_map/pallas_call | solution.py:370
  57.8 0.7 %copy.15 = bf16[4,6,16,384]{3,2,1,0:T(8,128)(2,1)} copy(bf16[4,6,16,384]{3,2,1,0:T(8,128)(2,1)S(1)} %bitcast.12) | data formatting | bytes 589824
  (7 shorter events, 0.1 us)
Async XLA Ops:
  0.0 5.9 %copy-start.2 = (bf16[27,24,384]{2,1,0:T(8,128)(2,1)S(1)}, bf16[27,24,384]{2,1,0:T(8,128)(2,1)}, u32[]{:S(2)}) copy-start(bf16[27,24,384]{2,1,0:T(8,128)(2,1)} %param.13) | copy-start | bytes 1492996
  1.0 4.9 %collective-permute-start = (bf16[7,24,384]{2,1,0:T(8,128)(2,1)S(1)}, bf16[7,24,384]{2,1,0:T(8,128)(2,1)S(1)}, u32[]{:S(2)}, u32[]{:S(2)}) collective-permute-start(bf16[7,24,384]{2,1,0:T(8,128)(2,1)S(1)} %pad_dynamic-slice_fusion), channel_id=1, source_target_pairs={{0,1},{1,0},{2,3},{3,2},{4,5},{5,4},{6,7},{7,6},{8,9},{9,8},{10,11... | collective-permute-start | bytes 387080 | tf_op jit(solution)/shard_map/ppermute | solution.py:352
  1.1 0.7 %copy-start.4 = (s32[8]{0:T(128)S(1)}, s32[8]{0:T(128)}, u32[]{:S(2)}) copy-start(s32[8]{0:T(128)} %param.9) | copy-start | bytes 100
  1.1 4.7 %copy-start.3 = (bf16[16,384]{1,0:T(8,128)(2,1)S(1)}, bf16[16,384]{1,0:T(8,128)(2,1)}, u32[]{:S(2)}) copy-start(bf16[16,384]{1,0:T(8,128)(2,1)} %param.8) | copy-start | bytes 36868
  3.7 0.7 %copy-start.5 = (f32[384]{0:T(512)S(1)}, f32[384]{0:T(512)}, u32[]{:S(2)}) copy-start(f32[384]{0:T(512)} %param.11) | copy-start | bytes 4612
  4.4 0.7 %copy-start.6 = (f32[384]{0:T(512)S(1)}, f32[384]{0:T(512)}, u32[]{:S(2)}) copy-start(f32[384]{0:T(512)} %param.12) | copy-start | bytes 4612
  5.1 0.7 %copy-start.7 = (f32[384]{0:T(512)S(1)}, f32[384]{0:T(512)}, u32[]{:S(2)}) copy-start(f32[384]{0:T(512)} %param.14) | copy-start | bytes 4612
  6.0 1.0 %copy-start = (bf16[27,16,384]{2,1,0:T(8,128)(2,1)S(1)}, bf16[27,16,384]{2,1,0:T(8,128)(2,1)}, u32[]{:S(2)}) copy-start(bf16[27,16,384]{2,1,0:T(8,128)(2,1)} %param.10) | copy-start | bytes 995332
  6.0 1.0 %copy-start.1 = (bf16[256,256]{1,0:T(8,128)(2,1)S(1)}, bf16[256,256]{1,0:T(8,128)(2,1)}, u32[]{:S(2)}) copy-start(bf16[256,256]{1,0:T(8,128)(2,1)} %constant.51.clone.perm) | copy-start | bytes 393220

commit v2 on v1

--- a/solution.py
+++ b/solution.py
@@ -1,6 +1,5 @@
 import jax
 import jax.numpy as jnp
-import numpy as np
 from jax import lax
 from jax.experimental import pallas as pl
 from jax.experimental.pallas import tpu as pltpu
@@ -101,9 +100,9 @@
 
 
 def section_kernel(
-    latq, perm, mask, entry, entry_bias, gain, residual_bias, pieces,
+    latq, counts, entry_far, entry_bias_far, gain_far, residual_bias_far, pieces,
     out,
-    lat, at, act, kept, weights, acc, done,
+    entry, entry_bias, gain, residual_bias, lat, at, act, kept, weights, acc, done,
     lat_send, lat_recv, z_send, z_recv, p_send, p_recv, c_send, c_recv, o_send, o_recv, own,
 ):
     x = lax.axis_index("groups")
@@ -150,21 +149,25 @@
             pieces.at[0], weights.at[quarter, :, rows_of(zz, y), :], z_send.at[0], z_recv.at[zz], where_(zz, y, c)
         )
 
-    def p_copy(r, zz):
+    def p_copy(r, zz, source=None):
         block = weights.at[quarter, :, rows_of(zz, y), :]
-        return remote(block, block, p_send.at[r, zz], p_recv.at[r, zz], peers[r])
+        return remote(block if source is None else source, block, p_send.at[r, zz], p_recv.at[r, zz], peers[r])
 
     def p_arrival(r, zz):
         block = weights.at[quarter if r == 0 else across, :, rows_of(zz, y if r == 1 else 1 - y), :]
         return remote(block, block, p_send.at[r, zz], p_recv.at[r, zz], peers[r])
 
-    def c_copy(i):
-        block = weights.at[quarter if i == 0 else across]
-        return remote(block, block, c_send.at[i], c_recv.at[i], sibling)
-
-    def c_arrival(i):
-        block = weights.at[2 * x + 1 - c if i == 0 else 2 * (1 - x) + 1 - c]
-        return remote(block, block, c_send.at[i], c_recv.at[i], sibling)
+    def c_block(core, r, zz):
+        which = 2 * (x if r < 2 else 1 - x) + core
+        return weights.at[which, :, rows_of(zz, y if r % 2 == 0 else 1 - y), :]
+
+    def c_copy(r, zz, source=None):
+        block = c_block(c, r, zz)
+        return remote(block if source is None else source, block, c_send.at[r, zz], c_recv.at[r, zz], sibling)
+
+    def c_arrival(r, zz):
+        block = c_block(1 - c, r, zz)
+        return remote(block, block, c_send.at[r, zz], c_recv.at[r, zz], sibling)
 
     def columns(n):
         return pl.ds(pl.multiple_of(128 * n, 128), 128)
@@ -187,22 +190,46 @@
 
     @pl.when(z < SLICES)
     def _():
+        own_piece = pieces.at[lax.rem(z, SLICES)]
+        for r in range(3):
+            p_copy(r, z, own_piece).start()
+        c_copy(0, z, own_piece).start()
         mine = [
             pltpu.make_async_copy(latq.at[me % 4], lat.at[me], own.at[0]),
-            pltpu.make_async_copy(pieces.at[lax.rem(z, SLICES)], weights.at[quarter, :, rows_of(z, y), :], own.at[1]),
+            pltpu.make_async_copy(own_piece, weights.at[quarter, :, rows_of(z, y), :], own.at[1]),
+            pltpu.make_async_copy(entry_far, entry, own.at[2]),
+            pltpu.make_async_copy(entry_bias_far, entry_bias, own.at[3]),
+            pltpu.make_async_copy(gain_far, gain, own.at[4]),
+            pltpu.make_async_copy(residual_bias_far, residual_bias, own.at[5]),
         ]
         for copy in mine:
             copy.start()
+
+        def forward(step):
+            near = jnp.where(z == 2, 3 - step, step + jnp.where(step >= z, 1, 0))
+            near = jnp.where((z == 2) & (step == 0), 3, near)
+            near = jnp.where((z == 2) & (step > 0), 2 - step, near)
+            z_arrival(near).wait_recv()
+            for r in range(3):
+                p_copy(r, near).start()
+            c_copy(0, near).start()
+
         at[:, 0:2] = jnp.zeros((2, 2, 144, PLANE), BF16)
         act[:, :, 0:2] = jnp.zeros((3, 2, 2, PLANE, C), BF16)
         act[:, :, 2:, 0:16] = jnp.zeros((3, 2, 8, 16, C), BF16)
         act[:, :, 2:, 112:128] = jnp.zeros((3, 2, 8, 16, C), BF16)
-        mine[0].wait()
+        forward(0)
+        for copy in mine:
+            copy.wait()
         for source in range(16):
             @pl.when(source != me)
             def _():
                 remote(latq.at[0], lat.at[source], lat_send.at[0], lat_recv.at[source], {"tm": source}).wait_recv()
-        cells = jnp.dot(perm[...], lat[...].reshape(256, PLANE), preferred_element_type=F32)
+        target = lax.broadcasted_iota(jnp.int32, (256, 256), 0)
+        origin = lax.broadcasted_iota(jnp.int32, (256, 256), 1)
+        h_, b_, g_, ch_ = target // 128, (target // 64) % 2, (target // 16) % 4, target % 16
+        perm = (origin == (g_ * 4 + ch_ // 4) * 16 + (b_ * 2 + h_) * 4 + ch_ % 4).astype(F32).astype(BF16)
+        cells = jnp.dot(perm, lat[...].reshape(256, PLANE), preferred_element_type=F32)
         lane = lax.broadcasted_iota(jnp.int32, (256, PLANE), 1)
         row, column = lane // LATENT_COLUMNS, lane % LATENT_COLUMNS
         for j in range(3):
@@ -224,11 +251,11 @@
             h, f = index // 8, index % 8
             left = at[h, pl.ds(f, 3)].reshape(432, PLANE)
             wide = lax.dot_general(left, entry[...], (((0,), (0,)), ((), ())), preferred_element_type=F32)
-            stream = (wide[:CELLS] + entry_bias[...]).astype(BF16)
+            stream = (wide[:CELLS] + entry_bias[...][None, :]).astype(BF16)
             kept[index] = stream
             values = stream.astype(F32)
             scale = lax.rsqrt(jnp.mean(values * values, axis=-1, keepdims=True) + 1e-06)
-            u = values * scale * gain[...]
+            u = values * scale * gain[...][None, :]
             active = (u / (1.0 + jnp.exp(-u))).astype(BF16).astype(F32)
             column = lax.broadcasted_iota(jnp.int32, (CELLS, C), 0) % LATENT_COLUMNS
             act[1, h, 2 + f, 16:112] = active.astype(BF16)
@@ -238,15 +265,11 @@
             ).astype(BF16)
             return carry
 
-        lax.fori_loop(0, 8, inlet, 0)
-        mine[1].wait()
-        for zz in range(4):
-            @pl.when(zz != z)
-            def _():
-                z_arrival(zz).wait_recv()
-            for r in range(3):
-                p_copy(r, zz).start()
-        lax.fori_loop(8, 16, inlet, 0)
+        lax.fori_loop(0, 4, inlet, 0)
+        forward(1)
+        lax.fori_loop(4, 10, inlet, 0)
+        forward(2)
+        lax.fori_loop(10, 16, inlet, 0)
 
         def taps_of(which, d):
             h, b = d % 2, d // 2
@@ -271,24 +294,29 @@
 
         for zz in range(4):
             p_arrival(0, zz).wait_recv()
-        c_copy(0).start()
+            c_copy(1, zz).start()
         sweep(quarter, True)
-        for r in (1, 2):
+        for zz in range(4):
+            for r in (1, 2):
+                p_arrival(r, zz).wait_recv()
+                c_copy(1 + r, zz).start()
+        for r in (0, 1):
             for zz in range(4):
-                p_arrival(r, zz).wait_recv()
-        c_copy(1).start()
-        c_arrival(0).wait_recv()
+                c_arrival(r, zz).wait_recv()
         sweep(2 * x + 1 - c, False)
         sweep(across, False)
-        c_arrival(1).wait_recv()
+        for r in (2, 3):
+            for zz in range(4):
+                c_arrival(r, zz).wait_recv()
         last = 2 * (1 - x) + 1 - c
 
         def finish(d, carry):
             h, b = d % 2, d // 2
             total = lax.fori_loop(0, TAPS, taps_of(last, d), acc[d], unroll=True)
             stream = kept[pl.ds(h * 8 + b * 4, 4), :, columns(z)].astype(F32)
-            total = stream + (total + residual_bias[0:1, columns(z)]).reshape(4, CELLS, 128)
-            valid = mask[pl.ds(h * 8 + b * 4, 4)] > 0.0
+            total = stream + (total + residual_bias[columns(z)][None, :]).reshape(4, CELLS, 128)
+            limit = counts[me % 4 + 4 * h]
+            valid = lax.broadcasted_iota(jnp.int32, (4, CELLS, 128), 0) + 4 * b < limit
             done[d] = jnp.where(valid, total, 0.0).astype(BF16).reshape(4 * CELLS, 128)
 
             @pl.when(d != z)
@@ -316,23 +344,13 @@
         for r in range(3):
             for zz in range(4):
                 p_copy(r, zz).wait_send()
-        for i in range(2):
-            c_copy(i).wait_send()
+        for r in range(4):
+            for zz in range(4):
+                c_copy(r, zz).wait_send()
         for d in range(4):
             @pl.when(d != z)
             def _():
                 o_copy(d).wait_send()
-
-
-def permutation():
-    matrix = np.zeros((256, 256), np.float32)
-    for h in range(2):
-        for b in range(2):
-            for g in range(4):
-                for ch in range(16):
-                    source = (g * 4 + ch // 4) * 16 + (b * 2 + h) * 4 + ch % 4
-                    matrix[(h * 8 + b * 4 + g) * 16 + ch, source] = 1.0
-    return matrix
 
 
 def sliced_shards(
@@ -357,22 +375,17 @@
 
     latq = jnp.transpose(sharded_latents.reshape(4, 4, 4, CELLS), (1, 0, 2, 3)).reshape(4, 16, CELLS)
     latq = jnp.pad(latq, ((0, 0), (0, 0), (0, PLANE - CELLS)))
-    q = me % 4
-    counts = jnp.stack([
-        lax.dynamic_index_in_dim(sample_frame_count, q, keepdims=False),
-        lax.dynamic_index_in_dim(sample_frame_count, q + 4, keepdims=False),
-    ])
-    mask = (jnp.arange(8)[None, :] < counts[:, None]).astype(F32).reshape(16, 1, 1)
-    mask = jnp.broadcast_to(mask, (16, 1, 128))
-
     vmem = pl.BlockSpec(memory_space=pltpu.VMEM)
+    far = pl.BlockSpec(memory_space=pltpu.HBM)
     dma = pltpu.SemaphoreType.DMA
     out = pl.pallas_call(
         section_kernel,
         out_shape=jax.ShapeDtypeStruct((4 * CELLS, C), BF16),
-        in_specs=[vmem] * 8,
+        in_specs=[vmem, pl.BlockSpec(memory_space=pltpu.SMEM)] + [far] * 4 + [vmem],
         out_specs=vmem,
         scratch_shapes=[
+            pltpu.VMEM((27 * LATENT_CHANNELS, C), BF16),
+            pltpu.VMEM((C,), F32), pltpu.VMEM((C,), F32), pltpu.VMEM((C,), F32),
             pltpu.VMEM((16, 16, PLANE), BF16),
             pltpu.VMEM((2, 10, 144, PLANE), BF16),
             pltpu.VMEM((3, 2, 10, PLANE, C), BF16),
@@ -381,7 +394,7 @@
             pltpu.VMEM((4, 4 * CELLS, 128), F32),
             pltpu.VMEM((4, 4 * CELLS, 128), BF16),
             dma((12,)), dma((16,)), dma((3,)), dma((4,)), dma((3, 4)), dma((3, 4)),
-            dma((2,)), dma((2,)), dma((4,)), dma((3,)), dma((2,)),
+            dma((4, 4)), dma((4, 4)), dma((4,)), dma((3,)), dma((6,)),
         ],
         compiler_params=pltpu.CompilerParams(
             collective_id=0, has_side_effects=True, vmem_limit_bytes=40 * 1024 * 1024
@@ -389,12 +402,11 @@
         cost_estimate=pl.CostEstimate(flops=5_000_000_000, bytes_accessed=2_000_000, transcendentals=600_000),
     )(
         latq,
-        jnp.asarray(permutation(), BF16),
-        mask,
+        sample_frame_count,
         entry_kernel.reshape(27 * LATENT_CHANNELS, C),
-        entry_bias.reshape(1, C),
-        norm_scale_gain.reshape(1, C),
-        residual_bias.reshape(1, C),
+        entry_bias,
+        norm_scale_gain,
+        residual_bias,
         pieces,
     )
     return out.reshape(4, LATENT_ROWS, LATENT_COLUMNS, C)

time: 58.8 us -> 47.9 us (0.81)
  Pallas kernels: 50.8 us -> 43.6 us
  local copies, waits for them, and re-layouts: 5.97 us -> 2.7 us
  other arithmetic: 1.51 us -> 0.08 us
  waiting for transfers between devices: 0.01 us -> 1.19 us
    pallas_call x1, Pallas kernels: 50.8 us -> 43.6 us  [sliced_shards(): pl.pallas_call(section_kernel, out_shape=jax.ShapeDtypeStruct((4 * CELLS,...]
    unnamed x17 -> x15, local copies, waits for them, and re-layouts: 4.11 us -> 1.62 us
    another operation x1 -> x0, other arithmetic: 1.35 us -> none  [sliced_shards(): jnp.stack([lax.dynamic_index_in_dim(sample_frame_count, q, keepdims=False...]
    ppermute x1, waiting for transfers between devices: 0.01 us -> 1.19 us  [sliced_shards(): received = lax.ppermute(theirs, 'tm', [(i, i ^ 1) for i in range(16)])]
    dynamic_slice x1 -> x0, local copies, waits for them, and re-layouts: 0.61 us -> none  [sliced_shards(): lax.dynamic_index_in_dim(sample_frame_count, q, keepdims=False)]
  transfers between devices with their start and end apart: 1 -> 1, of which waited for: 0 -> 1; matrix products, arithmetic and copies ran while one was open for 4% -> 0% of each run, Pallas kernels for 0% -> 0%
where the time goes in v2:
time: 47.9 us; the launch traced here: 47.8 us
  Pallas kernels  43.6 us (91%)
  local copies, waits for them, and re-layouts  2.7 us (6%)
  waiting for transfers between devices  1.19 us (2%)
    pallas_call x1, Pallas kernels, sliced_shards(): pl.pallas_call(section_kernel, out_shape=jax.ShapeDtypeStruct((4 * CELLS,...  43.6 us
    unnamed x15, local copies, waits for them, and re-layouts  1.62 us
    ppermute x1, waiting for transfers between devices, sliced_shards(): received = lax.ppermute(theirs, 'tm', [(i, i ^ 1) for i in range(16)])  1.19 us
    dynamic_slice x1, local copies, waits for them, and re-layouts, sliced_shards(): theirs = lax.dynamic_slice_in_dim(quarters, (2 * x + 1 - c) * TAPS, TAPS, 0)  0.98 us
  transfers between devices with their start and end apart: 1, of which 1 were waited for; matrix products, arithmetic and copies ran while one was open for 0% of the time, Pallas kernels for 0%

profile of v2, /device:TPU:26, one launch (start us, length us, event | category | flops | bytes accessed | tf_op | source)
XLA Modules:
  0.0 47.8 jit_solution(15421833136383719358)
XLA Ops:
  0.0 0.0 copy-start.5
  0.0 0.0 copy-start.6
  0.0 1.0 %pad_dynamic-slice_fusion = bf16[7,24,384]{2,1,0:T(8,128)(2,1)S(1)} fusion(s32[]{:T(128)S(6)} %select_n.28, bf16[27,24,384]{2,1,0:T(8,128)(2,1)} %param.12), kind=kLoop, calls=%fused_computation | loop fusion | bytes 626692 | tf_op jit(solution)/shard_map/dynamic_slice | solution.py:369
  1.0 0.1 collective-permute-start
  1.1 0.0 copy-done.6
  1.1 0.1 reshape.15
  1.2 1.2 %collective-permute-done = bf16[7,24,384]{2,1,0:T(8,128)(2,1)S(1)} collective-permute-done((bf16[7,24,384]{2,1,0:T(8,128)(2,1)S(1)}, bf16[7,24,384]{2,1,0:T(8,128)(2,1)S(1)}, u32[]{:S(2)}, u32[]{:S(2)}) %collective-permute-start) | collective-permute-done | bytes 129056 | tf_op jit(solution)/shard_map/ppermute | solution.py:370
  2.4 0.0 copy-done.5
  2.4 0.0 copy-start
  2.5 0.0 copy-start.1
  2.5 0.0 copy-start.2
  2.5 0.0 copy-start.3
  2.5 0.0 copy-start.4
  2.6 0.9 %copy-done = bf16[27,16,384]{2,1,0:T(8,128)(2,1)S(1)} copy-done((bf16[27,16,384]{2,1,0:T(8,128)(2,1)S(1)}, bf16[27,16,384]{2,1,0:T(8,128)(2,1)}, u32[]{:S(2)}) %copy-start) | copy-done | bytes 331800
  3.4 0.0 copy-done.1
  3.4 0.0 copy-done.2
  3.4 0.0 copy-done.3
  3.4 0.0 copy-done.4
  3.4 43.6 %shard_map.73 = bf16[384,384]{1,0:T(8,128)(2,1)S(1)} custom-call(bf16[4,16,128]{2,1,0:T(8,128)(2,1)S(1)} %pad.8.latq, s32[8]{0:T(128)S(1)} %copy-done.4, bf16[432,384]{1,0:T(8,128)(2,1)S(1)} %bitcast.13, f32[384]{0:T(512)S(1)} %copy-done.1, f32[384]{0:T(512)S(1)} %copy-done.2, f32[384]{0:T(512)S(1)} %copy-done.3, ...), custom_call_target="tpu_custom_call" | custom-call | flops 5000000000 | bytes 2000000 | tf_op jit(solution)/shard_map/pallas_call | solution.py:381
  47.1 0.7 %copy.14 = bf16[4,6,16,384]{3,2,1,0:T(8,128)(2,1)} copy(bf16[4,6,16,384]{3,2,1,0:T(8,128)(2,1)S(1)} %bitcast.12) | data formatting | bytes 589824
  (4 shorter events, 0.1 us)
Async XLA Ops:
  0.0 2.4 %copy-start.5 = (bf16[27,24,384]{2,1,0:T(8,128)(2,1)S(1)}, bf16[27,24,384]{2,1,0:T(8,128)(2,1)}, u32[]{:S(2)}) copy-start(bf16[27,24,384]{2,1,0:T(8,128)(2,1)} %param.12) | copy-start | bytes 1492996
  0.0 1.1 %copy-start.6 = (bf16[16,384]{1,0:T(8,128)(2,1)S(1)}, bf16[16,384]{1,0:T(8,128)(2,1)}, u32[]{:S(2)}) copy-start(bf16[16,384]{1,0:T(8,128)(2,1)} %param.7) | copy-start | bytes 36868
  1.0 1.4 %collective-permute-start = (bf16[7,24,384]{2,1,0:T(8,128)(2,1)S(1)}, bf16[7,24,384]{2,1,0:T(8,128)(2,1)S(1)}, u32[]{:S(2)}, u32[]{:S(2)}) collective-permute-start(bf16[7,24,384]{2,1,0:T(8,128)(2,1)S(1)} %pad_dynamic-slice_fusion), channel_id=1, source_target_pairs={{0,1},{1,0},{2,3},{3,2},{4,5},{5,4},{6,7},{7,6},{8,9},{9,8},{10,11... | collective-permute-start | bytes 387080 | tf_op jit(solution)/shard_map/ppermute | solution.py:370
  2.4 1.0 %copy-start = (bf16[27,16,384]{2,1,0:T(8,128)(2,1)S(1)}, bf16[27,16,384]{2,1,0:T(8,128)(2,1)}, u32[]{:S(2)}) copy-start(bf16[27,16,384]{2,1,0:T(8,128)(2,1)} %param.9) | copy-start | bytes 995332
  2.5 1.0 %copy-start.1 = (f32[384]{0:T(512)S(1)}, f32[384]{0:T(512)}, u32[]{:S(2)}) copy-start(f32[384]{0:T(512)} %entry_bias_far.1) | copy-start | bytes 4612
  2.5 1.0 %copy-start.2 = (f32[384]{0:T(512)S(1)}, f32[384]{0:T(512)}, u32[]{:S(2)}) copy-start(f32[384]{0:T(512)} %gain_far.1) | copy-start | bytes 4612
  2.5 0.9 %copy-start.3 = (f32[384]{0:T(512)S(1)}, f32[384]{0:T(512)}, u32[]{:S(2)}) copy-start(f32[384]{0:T(512)} %residual_bias_far.1) | copy-start | bytes 4612
  2.5 0.9 %copy-start.4 = (s32[8]{0:T(128)S(1)}, s32[8]{0:T(128)}, u32[]{:S(2)}) copy-start(s32[8]{0:T(128)} %counts.1) | copy-start | bytes 100

commit v3 on v2

--- a/solution.py
+++ b/solution.py
@@ -271,23 +271,23 @@
         forward(2)
         lax.fori_loop(10, 16, inlet, 0)
 
-        def taps_of(which, d):
+        def taps_of(which, d, total):
             h, b = d % 2, d // 2
-
-            def step(t, total):
-                tap = jnp.minimum(which * TAPS + t, 26)
-                i, j, k = tap // 9, (tap // 3) % 3, tap % 3
-                left = act[k, h, pl.ds(4 * b + i, 4), pl.ds(pl.multiple_of(16 * j, 16), CELLS), :]
-                return total + jnp.dot(
-                    left.reshape(4 * CELLS, C), weights[which, t], preferred_element_type=F32
-                )
-
-            return step
+            for low, count in ((0, 7),):
+                lefts = []
+                for t in range(low, low + count):
+                    tap = jnp.minimum(which * TAPS + t, 26)
+                    i, j, k = tap // 9, (tap // 3) % 3, tap % 3
+                    left = act[k, h, pl.ds(4 * b + i, 4), pl.ds(pl.multiple_of(16 * j, 16), CELLS), :]
+                    lefts.append(left.reshape(4 * CELLS, C))
+                right = weights[which, low : low + count].reshape(count * C, 128)
+                total = total + jnp.dot(jnp.concatenate(lefts, axis=1), right, preferred_element_type=F32)
+            return total
 
         def sweep(which, first):
             def body(d, carry):
                 start = jnp.zeros((4 * CELLS, 128), F32) if first else acc[d]
-                acc[d] = lax.fori_loop(0, TAPS, taps_of(which, d), start, unroll=True)
+                acc[d] = taps_of(which, d, start)
                 return carry
 
             lax.fori_loop(0, 4, body, 0)
@@ -310,9 +310,12 @@
                 c_arrival(r, zz).wait_recv()
         last = 2 * (1 - x) + 1 - c
 
-        def finish(d, carry):
+        def finish(step, carry):
+            middle = jnp.where(step == 0, 3, jnp.where(step == 1, 0, jnp.where(step == 2, 2, 1)))
+            upper = jnp.where(step < 2, step, 5 - step)
+            d = jnp.where(z == 0, 3 - step, jnp.where(z == 1, middle, upper))
             h, b = d % 2, d // 2
-            total = lax.fori_loop(0, TAPS, taps_of(last, d), acc[d], unroll=True)
+            total = taps_of(last, d, acc[d])
             stream = kept[pl.ds(h * 8 + b * 4, 4), :, columns(z)].astype(F32)
             total = stream + (total + residual_bias[columns(z)][None, :]).reshape(4, CELLS, 128)
             limit = counts[me % 4 + 4 * h]

time: 47.9 us -> 46.7 us (0.975)
  the two profiles are of different devices: /device:TPU:26 before, /device:TPU:18 now
where the time goes in v3:
time: 46.7 us; the launch traced here: 46.5 us
  Pallas kernels  42.4 us (91%)
  local copies, waits for them, and re-layouts  2.7 us (6%)
  waiting for transfers between devices  1.19 us (3%)
    pallas_call x1, Pallas kernels, sliced_shards(): pl.pallas_call(section_kernel, out_shape=jax.ShapeDtypeStruct((4 * CELLS,...  42.4 us
    unnamed x15, local copies, waits for them, and re-layouts  1.62 us
    ppermute x1, waiting for transfers between devices, sliced_shards(): received = lax.ppermute(theirs, 'tm', [(i, i ^ 1) for i in range(16)])  1.19 us
    dynamic_slice x1, local copies, waits for them, and re-layouts, sliced_shards(): theirs = lax.dynamic_slice_in_dim(quarters, (2 * x + 1 - c) * TAPS, TAPS, 0)  0.98 us
  transfers between devices with their start and end apart: 1, of which 1 were waited for; matrix products, arithmetic and copies ran while one was open for 0% of the time, Pallas kernels for 0%

profile of v3, /device:TPU:18, one launch (start us, length us, event | category | flops | bytes accessed | tf_op | source)
XLA Modules:
  0.0 46.5 jit_solution(1400959691221625861)
XLA Ops:
  0.0 0.0 copy-start.5
  0.0 0.0 copy-start.6
  0.0 1.0 %pad_dynamic-slice_fusion = bf16[7,24,384]{2,1,0:T(8,128)(2,1)S(1)} fusion(s32[]{:T(128)S(6)} %select_n.28, bf16[27,24,384]{2,1,0:T(8,128)(2,1)} %param.12), kind=kLoop, calls=%fused_computation | loop fusion | bytes 626692 | tf_op jit(solution)/shard_map/dynamic_slice | solution.py:372
  1.0 0.1 collective-permute-start
  1.1 0.0 copy-done.6
  1.1 0.1 reshape.15
  1.2 1.2 %collective-permute-done = bf16[7,24,384]{2,1,0:T(8,128)(2,1)S(1)} collective-permute-done((bf16[7,24,384]{2,1,0:T(8,128)(2,1)S(1)}, bf16[7,24,384]{2,1,0:T(8,128)(2,1)S(1)}, u32[]{:S(2)}, u32[]{:S(2)}) %collective-permute-start) | collective-permute-done | bytes 129056 | tf_op jit(solution)/shard_map/ppermute | solution.py:373
  2.4 0.0 copy-done.5
  2.4 0.0 copy-start
  2.5 0.0 copy-start.1
  2.5 0.0 copy-start.2
  2.5 0.0 copy-start.3
  2.5 0.0 copy-start.4
  2.6 0.9 %copy-done = bf16[27,16,384]{2,1,0:T(8,128)(2,1)S(1)} copy-done((bf16[27,16,384]{2,1,0:T(8,128)(2,1)S(1)}, bf16[27,16,384]{2,1,0:T(8,128)(2,1)}, u32[]{:S(2)}) %copy-start) | copy-done | bytes 331800
  3.4 0.0 copy-done.1
  3.4 0.0 copy-done.2
  3.4 0.0 copy-done.3
  3.4 0.0 copy-done.4
  3.4 42.4 %shard_map.73 = bf16[384,384]{1,0:T(8,128)(2,1)S(1)} custom-call(bf16[4,16,128]{2,1,0:T(8,128)(2,1)S(1)} %pad.8.latq, s32[8]{0:T(128)S(1)} %copy-done.4, bf16[432,384]{1,0:T(8,128)(2,1)S(1)} %bitcast.13, f32[384]{0:T(512)S(1)} %copy-done.1, f32[384]{0:T(512)S(1)} %copy-done.2, f32[384]{0:T(512)S(1)} %copy-done.3, ...), custom_call_target="tpu_custom_call" | custom-call | flops 5000000000 | bytes 2000000 | tf_op jit(solution)/shard_map/pallas_call | solution.py:384
  45.8 0.7 %copy.14 = bf16[4,6,16,384]{3,2,1,0:T(8,128)(2,1)} copy(bf16[4,6,16,384]{3,2,1,0:T(8,128)(2,1)S(1)} %bitcast.12) | data formatting | bytes 589824
  (4 shorter events, 0.1 us)
Async XLA Ops:
  0.0 2.4 %copy-start.5 = (bf16[27,24,384]{2,1,0:T(8,128)(2,1)S(1)}, bf16[27,24,384]{2,1,0:T(8,128)(2,1)}, u32[]{:S(2)}) copy-start(bf16[27,24,384]{2,1,0:T(8,128)(2,1)} %param.12) | copy-start | bytes 1492996
  0.0 1.1 %copy-start.6 = (bf16[16,384]{1,0:T(8,128)(2,1)S(1)}, bf16[16,384]{1,0:T(8,128)(2,1)}, u32[]{:S(2)}) copy-start(bf16[16,384]{1,0:T(8,128)(2,1)} %param.7) | copy-start | bytes 36868
  1.0 1.4 %collective-permute-start = (bf16[7,24,384]{2,1,0:T(8,128)(2,1)S(1)}, bf16[7,24,384]{2,1,0:T(8,128)(2,1)S(1)}, u32[]{:S(2)}, u32[]{:S(2)}) collective-permute-start(bf16[7,24,384]{2,1,0:T(8,128)(2,1)S(1)} %pad_dynamic-slice_fusion), channel_id=1, source_target_pairs={{0,1},{1,0},{2,3},{3,2},{4,5},{5,4},{6,7},{7,6},{8,9},{9,8},{10,11... | collective-permute-start | bytes 387080 | tf_op jit(solution)/shard_map/ppermute | solution.py:373
  2.4 1.0 %copy-start = (bf16[27,16,384]{2,1,0:T(8,128)(2,1)S(1)}, bf16[27,16,384]{2,1,0:T(8,128)(2,1)}, u32[]{:S(2)}) copy-start(bf16[27,16,384]{2,1,0:T(8,128)(2,1)} %param.9) | copy-start | bytes 995332
  2.5 1.0 %copy-start.1 = (f32[384]{0:T(512)S(1)}, f32[384]{0:T(512)}, u32[]{:S(2)}) copy-start(f32[384]{0:T(512)} %entry_bias_far.1) | copy-start | bytes 4612
  2.5 1.0 %copy-start.2 = (f32[384]{0:T(512)S(1)}, f32[384]{0:T(512)}, u32[]{:S(2)}) copy-start(f32[384]{0:T(512)} %gain_far.1) | copy-start | bytes 4612
  2.5 0.9 %copy-start.3 = (f32[384]{0:T(512)S(1)}, f32[384]{0:T(512)}, u32[]{:S(2)}) copy-start(f32[384]{0:T(512)} %residual_bias_far.1) | copy-start | bytes 4612
  2.5 0.9 %copy-start.4 = (s32[8]{0:T(128)S(1)}, s32[8]{0:T(128)}, u32[]{:S(2)}) copy-start(s32[8]{0:T(128)} %counts.1) | copy-start | bytes 100
